TPU v7x, 32 devices: a whole 2x2x4 slice. The times are simulated.
32 devices in a mesh: seq: 16 (over z, y, core), head: 2 (over x).
Axes of the slice: x: 2, y: 2, z: 4, core: 2. Of those that a mesh axis runs over, the one named last changes fastest.
Arguments:
- query: bfloat16 [8192, 32, 128], P('seq', 'head'), may hold values from -6 to 6
- key: bfloat16 [8192, 16, 128], P('seq', 'head'), may hold values from -6 to 6
- value: bfloat16 [8192, 16, 128], P('seq', 'head'), may hold values from -6 to 6
- grad_out: bfloat16 [8192, 32, 128], P('seq', 'head'), may hold values from -25 to 25
- q_gain: float32 [128], replicated, may hold values from 0.1 to 1.9
- k_gain: float32 [128], replicated, may hold values from 0.1 to 1.9
Outputs:
- grad_query: bfloat16 [8192, 32, 128], P('seq', 'head')
- grad_key: bfloat16 [8192, 16, 128], P('seq', 'head')
- grad_value: bfloat16 [8192, 16, 128], P('seq', 'head')
- grad_q_gain: float32 [128], replicated
- grad_k_gain: float32 [128], replicated
All inputs are finite; a program needn't handle non-finite values.
Results may differ from a plain program's by a relative error of at most 0.0099.
Values may be sent and summed in bfloat16 or wider, within the bound.
No kernel may reach another device: no remote copies, remote signals or barrier semaphores. Data moves between devices by JAX's collectives and lax.ppermute only.
A program may use at most 128 MiB of HBM per device.

v0:
```python
import jax
import jax.numpy as jnp
from jax import lax
from jax.sharding import PartitionSpec as P

WINDOW = 1024


score_scale = 168.0 ** (-0.5)
norm_eps = 1e-06


def passed_along(value, axis, steps):
    count = lax.axis_size(axis)
    initial, last = (max(0, -steps), min(count, count - steps))
    return lax.ppermute(value, axis, [(source, source + steps) for source in range(initial, last)])


def normalize(inputs_raw, gain_vec):
    as_float = inputs_raw.astype(jnp.float32)
    inverse_rms = lax.rsqrt(jnp.mean(as_float * as_float, axis=-1, keepdims=True) + norm_eps)
    unit_rows = as_float * inverse_rms
    return (unit_rows * gain_vec, unit_rows, inverse_rms)


def norm_back(d_normed, unit_rows, inverse_rms, gain_vec):
    d_unit = d_normed * gain_vec
    d_inputs = inverse_rms * (
        d_unit - unit_rows * jnp.mean(d_unit * unit_rows, axis=-1, keepdims=True)
    )
    d_gain = jnp.sum(d_normed * unit_rows, axis=(0, 1))
    return (d_inputs, d_gain)


def head_grads(query_head, key_head, value_head, incoming_gradient, allowed):
    last_last = (((1,), (1,)), ((), ()))
    first_first = (((0,), (0,)), ((), ()))
    scores = score_scale * lax.dot_general(
        query_head, key_head, last_last, preferred_element_type=jnp.float32
    )
    exp_scores = jnp.where(allowed, jnp.exp(scores), 0.0)
    attn_probs = exp_scores / jnp.sum(exp_scores, axis=1, keepdims=True)
    probs_low = attn_probs.astype(jnp.bfloat16)
    attended = jnp.dot(probs_low, value_head, preferred_element_type=jnp.float32)
    offset = jnp.sum(incoming_gradient.astype(jnp.float32) * attended, axis=1, keepdims=True)
    d_probs = lax.dot_general(
        incoming_gradient, value_head, last_last, preferred_element_type=jnp.float32
    )
    d_scores = (attn_probs * (d_probs - offset)).astype(jnp.bfloat16)
    value_grad = lax.dot_general(
        probs_low, incoming_gradient, first_first, preferred_element_type=jnp.float32
    )
    query_grad = score_scale * jnp.dot(d_scores, key_head, preferred_element_type=jnp.float32)
    key_grad = score_scale * lax.dot_general(
        d_scores, query_head, first_first, preferred_element_type=jnp.float32
    )
    return (query_grad, key_grad, value_grad)


def per_device(query, key, value, grad_out, q_gain, k_gain):
    rows_dev, heads_dev, head_width = query.shape
    kv_dev = key.shape[1]
    heads_per_group = heads_dev // kv_dev
    reach_total = (WINDOW + rows_dev - 1) // rows_dev
    key_span = (reach_total + 1) * rows_dev
    shard_index = lax.axis_index("seq")
    q_normed, q_unit, q_inverse = normalize(query, q_gain)
    k_normed, k_unit, k_inverse = normalize(key, k_gain)
    query_low = q_normed.astype(jnp.bfloat16)
    key_low = k_normed.astype(jnp.bfloat16)
    earlier = [
        passed_along((key_low, value), "seq", distance) for distance in range(1, reach_total + 1)
    ]
    keys_all = jnp.concatenate([received[0] for received in earlier[::-1]] + [key_low], axis=0)
    values_all = jnp.concatenate([received[1] for received in earlier[::-1]] + [value], axis=0)
    row_ids = jnp.arange(rows_dev, dtype=jnp.int32)[:, None]
    col_ids = jnp.arange(key_span, dtype=jnp.int32)[None, :]
    distance_grid = row_ids + reach_total * rows_dev - col_ids
    allowed = (
        (distance_grid >= 0)
        & (distance_grid < WINDOW)
        & (col_ids + shard_index * rows_dev >= reach_total * rows_dev)
    )
    query_heads = jnp.transpose(query_low, (1, 0, 2))
    upstream_heads = jnp.transpose(grad_out, (1, 0, 2))

    def per_head(unused, inputs):
        head_id, query_head, incoming_gradient = inputs
        kv_index = head_id // heads_per_group
        key_head = lax.dynamic_index_in_dim(keys_all, kv_index, 1, keepdims=False)
        value_head = lax.dynamic_index_in_dim(values_all, kv_index, 1, keepdims=False)
        return (unused, head_grads(query_head, key_head, value_head, incoming_gradient, allowed))

    head_ids = jnp.arange(heads_dev, dtype=jnp.int32)
    unused, (query_parts, key_parts, value_parts) = lax.scan(
        per_head, 0, (head_ids, query_heads, upstream_heads)
    )
    query_grad_n = jnp.transpose(query_parts, (1, 0, 2))
    key_sum = jnp.transpose(
        key_parts.reshape(kv_dev, heads_per_group, key_span, head_width).sum(axis=1), (1, 0, 2)
    )
    value_sum = jnp.transpose(
        value_parts.reshape(kv_dev, heads_per_group, key_span, head_width).sum(axis=1), (1, 0, 2)
    )
    key_total = key_sum[0:rows_dev]
    value_total = value_sum[0:rows_dev]
    for distance in range(reach_total - 1, -1, -1):
        low_row = (reach_total - distance) * rows_dev
        key_total, value_total = passed_along((key_total, value_total), "seq", -1)
        key_total = key_total + key_sum[low_row : low_row + rows_dev]
        value_total = value_total + value_sum[low_row : low_row + rows_dev]
    grad_query, q_gain_part = norm_back(query_grad_n, q_unit, q_inverse, q_gain)
    grad_key, k_gain_part = norm_back(key_total, k_unit, k_inverse, k_gain)
    grad_q_gain, grad_k_gain = lax.psum((q_gain_part, k_gain_part), ("seq", "head"))
    return (
        grad_query.astype(jnp.bfloat16),
        grad_key.astype(jnp.bfloat16),
        value_total.astype(jnp.bfloat16),
        grad_q_gain,
        grad_k_gain,
    )


def solution(mesh):
    return jax.shard_map(
        per_device,
        mesh=mesh,
        in_specs=(
            P("seq", "head", None),
            P("seq", "head", None),
            P("seq", "head", None),
            P("seq", "head", None),
            P(),
            P(),
        ),
        out_specs=(
            P("seq", "head", None),
            P("seq", "head", None),
            P("seq", "head", None),
            P(),
            P(),
        ),
        check_vma=False,
    )
```

profile of v0, /device:TPU:0, one launch (start us, length us, event | category | flops | bytes accessed | tf_op | source)
XLA Modules:
  0.0 636.3 jit_solution(14331706682958620681)
XLA Ops:
  37.1 19.3 %collective-permute-done = bf16[512,8,128]{2,0,1:T(8,128)(2,1)} collective-permute-done((bf16[512,8,128]{2,0,1:T(8,128)(2,1)}, bf16[512,8,128]{2,0,1:T(8,128)(2,1)}, u32[]{:S(2)}, u32[]{:S(2)}) %collective-permute-start) | collective-permute-done | bytes 1048608 | tf_op jit(solution)/shard_map/ppermute | solution.py:16
  59.6 408.8 %while.17 = (s32[]{:T(128)}, f32[16,512,128]{2,0,1:T(8,128)}, f32[16,1536,128]{2,1,0:T(8,128)}, f32[16,1536,128]{2,1,0:T(8,128)}, bf16[16,512,128]{2,1,0:T(8,128...) while((s32[]{:T(128)}, f32[16,512,128]{2,0,1:T(8,128)}, ...), condition=%wide.region_5.6_spmd.clone, body=%wide.region_2.5_spmd.clone.sunk | while | flops 1221000192 | bytes 34490260 | solution.py:95
  71.1 8.1 %dynamic_update_slice.30 = f32[16,512,128]{2,0,1:T(8,128)} dynamic-update-slice(f32[16,512,128]{2,0,1:T(8,128)} %get-tuple-element.317, f32[1,512,128]{2,0,1:T(1,128)S(1)} %bitcast.89, s32[]{:T(128)S(6)} %copy.52, s32[]{:T(128)} %constant.87.clone.1..sunk, s32[]{:T(128)} %constant.87.clone.1..sunk) | dynamic-update-slice | bytes 524292 | tf_op jit(solution)/shard_map/while/body/jit(dynamic_update_index_in_dim)/dynamic_update_slice | solution.py:95
  96.7 8.1 %dynamic_update_slice.30 = f32[16,512,128]{2,0,1:T(8,128)} dynamic-update-slice(f32[16,512,128]{2,0,1:T(8,128)} %get-tuple-element.317, f32[1,512,128]{2,0,1:T(1,128)S(1)} %bitcast.89, s32[]{:T(128)S(6)} %copy.52, s32[]{:T(128)} %constant.87.clone.1..sunk, s32[]{:T(128)} %constant.87.clone.1..sunk) | dynamic-update-slice | bytes 524292 | tf_op jit(solution)/shard_map/while/body/jit(dynamic_update_index_in_dim)/dynamic_update_slice | solution.py:95
  122.2 8.1 %dynamic_update_slice.30 = f32[16,512,128]{2,0,1:T(8,128)} dynamic-update-slice(f32[16,512,128]{2,0,1:T(8,128)} %get-tuple-element.317, f32[1,512,128]{2,0,1:T(1,128)S(1)} %bitcast.89, s32[]{:T(128)S(6)} %copy.52, s32[]{:T(128)} %constant.87.clone.1..sunk, s32[]{:T(128)} %constant.87.clone.1..sunk) | dynamic-update-slice | bytes 524292 | tf_op jit(solution)/shard_map/while/body/jit(dynamic_update_index_in_dim)/dynamic_update_slice | solution.py:95
  147.7 8.1 %dynamic_update_slice.30 = f32[16,512,128]{2,0,1:T(8,128)} dynamic-update-slice(f32[16,512,128]{2,0,1:T(8,128)} %get-tuple-element.317, f32[1,512,128]{2,0,1:T(1,128)S(1)} %bitcast.89, s32[]{:T(128)S(6)} %copy.52, s32[]{:T(128)} %constant.87.clone.1..sunk, s32[]{:T(128)} %constant.87.clone.1..sunk) | dynamic-update-slice | bytes 524292 | tf_op jit(solution)/shard_map/while/body/jit(dynamic_update_index_in_dim)/dynamic_update_slice | solution.py:95
  173.3 8.1 %dynamic_update_slice.30 = f32[16,512,128]{2,0,1:T(8,128)} dynamic-update-slice(f32[16,512,128]{2,0,1:T(8,128)} %get-tuple-element.317, f32[1,512,128]{2,0,1:T(1,128)S(1)} %bitcast.89, s32[]{:T(128)S(6)} %copy.52, s32[]{:T(128)} %constant.87.clone.1..sunk, s32[]{:T(128)} %constant.87.clone.1..sunk) | dynamic-update-slice | bytes 524292 | tf_op jit(solution)/shard_map/while/body/jit(dynamic_update_index_in_dim)/dynamic_update_slice | solution.py:95
  198.8 8.1 %dynamic_update_slice.30 = f32[16,512,128]{2,0,1:T(8,128)} dynamic-update-slice(f32[16,512,128]{2,0,1:T(8,128)} %get-tuple-element.317, f32[1,512,128]{2,0,1:T(1,128)S(1)} %bitcast.89, s32[]{:T(128)S(6)} %copy.52, s32[]{:T(128)} %constant.87.clone.1..sunk, s32[]{:T(128)} %constant.87.clone.1..sunk) | dynamic-update-slice | bytes 524292 | tf_op jit(solution)/shard_map/while/body/jit(dynamic_update_index_in_dim)/dynamic_update_slice | solution.py:95
  224.3 8.1 %dynamic_update_slice.30 = f32[16,512,128]{2,0,1:T(8,128)} dynamic-update-slice(f32[16,512,128]{2,0,1:T(8,128)} %get-tuple-element.317, f32[1,512,128]{2,0,1:T(1,128)S(1)} %bitcast.89, s32[]{:T(128)S(6)} %copy.52, s32[]{:T(128)} %constant.87.clone.1..sunk, s32[]{:T(128)} %constant.87.clone.1..sunk) | dynamic-update-slice | bytes 524292 | tf_op jit(solution)/shard_map/while/body/jit(dynamic_update_index_in_dim)/dynamic_update_slice | solution.py:95
  249.9 8.1 %dynamic_update_slice.30 = f32[16,512,128]{2,0,1:T(8,128)} dynamic-update-slice(f32[16,512,128]{2,0,1:T(8,128)} %get-tuple-element.317, f32[1,512,128]{2,0,1:T(1,128)S(1)} %bitcast.89, s32[]{:T(128)S(6)} %copy.52, s32[]{:T(128)} %constant.87.clone.1..sunk, s32[]{:T(128)} %constant.87.clone.1..sunk) | dynamic-update-slice | bytes 524292 | tf_op jit(solution)/shard_map/while/body/jit(dynamic_update_index_in_dim)/dynamic_update_slice | solution.py:95
  275.5 8.1 %dynamic_update_slice.30 = f32[16,512,128]{2,0,1:T(8,128)} dynamic-update-slice(f32[16,512,128]{2,0,1:T(8,128)} %get-tuple-element.317, f32[1,512,128]{2,0,1:T(1,128)S(1)} %bitcast.89, s32[]{:T(128)S(6)} %copy.52, s32[]{:T(128)} %constant.87.clone.1..sunk, s32[]{:T(128)} %constant.87.clone.1..sunk) | dynamic-update-slice | bytes 524292 | tf_op jit(solution)/shard_map/while/body/jit(dynamic_update_index_in_dim)/dynamic_update_slice | solution.py:95
  301.1 8.1 %dynamic_update_slice.30 = f32[16,512,128]{2,0,1:T(8,128)} dynamic-update-slice(f32[16,512,128]{2,0,1:T(8,128)} %get-tuple-element.317, f32[1,512,128]{2,0,1:T(1,128)S(1)} %bitcast.89, s32[]{:T(128)S(6)} %copy.52, s32[]{:T(128)} %constant.87.clone.1..sunk, s32[]{:T(128)} %constant.87.clone.1..sunk) | dynamic-update-slice | bytes 524292 | tf_op jit(solution)/shard_map/while/body/jit(dynamic_update_index_in_dim)/dynamic_update_slice | solution.py:95
  326.6 8.1 %dynamic_update_slice.30 = f32[16,512,128]{2,0,1:T(8,128)} dynamic-update-slice(f32[16,512,128]{2,0,1:T(8,128)} %get-tuple-element.317, f32[1,512,128]{2,0,1:T(1,128)S(1)} %bitcast.89, s32[]{:T(128)S(6)} %copy.52, s32[]{:T(128)} %constant.87.clone.1..sunk, s32[]{:T(128)} %constant.87.clone.1..sunk) | dynamic-update-slice | bytes 524292 | tf_op jit(solution)/shard_map/while/body/jit(dynamic_update_index_in_dim)/dynamic_update_slice | solution.py:95
  352.1 8.1 %dynamic_update_slice.30 = f32[16,512,128]{2,0,1:T(8,128)} dynamic-update-slice(f32[16,512,128]{2,0,1:T(8,128)} %get-tuple-element.317, f32[1,512,128]{2,0,1:T(1,128)S(1)} %bitcast.89, s32[]{:T(128)S(6)} %copy.52, s32[]{:T(128)} %constant.87.clone.1..sunk, s32[]{:T(128)} %constant.87.clone.1..sunk) | dynamic-update-slice | bytes 524292 | tf_op jit(solution)/shard_map/while/body/jit(dynamic_update_index_in_dim)/dynamic_update_slice | solution.py:95
  377.7 8.1 %dynamic_update_slice.30 = f32[16,512,128]{2,0,1:T(8,128)} dynamic-update-slice(f32[16,512,128]{2,0,1:T(8,128)} %get-tuple-element.317, f32[1,512,128]{2,0,1:T(1,128)S(1)} %bitcast.89, s32[]{:T(128)S(6)} %copy.52, s32[]{:T(128)} %constant.87.clone.1..sunk, s32[]{:T(128)} %constant.87.clone.1..sunk) | dynamic-update-slice | bytes 524292 | tf_op jit(solution)/shard_map/while/body/jit(dynamic_update_index_in_dim)/dynamic_update_slice | solution.py:95
  403.3 8.1 %dynamic_update_slice.30 = f32[16,512,128]{2,0,1:T(8,128)} dynamic-update-slice(f32[16,512,128]{2,0,1:T(8,128)} %get-tuple-element.317, f32[1,512,128]{2,0,1:T(1,128)S(1)} %bitcast.89, s32[]{:T(128)S(6)} %copy.52, s32[]{:T(128)} %constant.87.clone.1..sunk, s32[]{:T(128)} %constant.87.clone.1..sunk) | dynamic-update-slice | bytes 524292 | tf_op jit(solution)/shard_map/while/body/jit(dynamic_update_index_in_dim)/dynamic_update_slice | solution.py:95
  428.8 8.1 %dynamic_update_slice.30 = f32[16,512,128]{2,0,1:T(8,128)} dynamic-update-slice(f32[16,512,128]{2,0,1:T(8,128)} %get-tuple-element.317, f32[1,512,128]{2,0,1:T(1,128)S(1)} %bitcast.89, s32[]{:T(128)S(6)} %copy.52, s32[]{:T(128)} %constant.87.clone.1..sunk, s32[]{:T(128)} %constant.87.clone.1..sunk) | dynamic-update-slice | bytes 524292 | tf_op jit(solution)/shard_map/while/body/jit(dynamic_update_index_in_dim)/dynamic_update_slice | solution.py:95
  454.4 8.1 %dynamic_update_slice.30 = f32[16,512,128]{2,0,1:T(8,128)} dynamic-update-slice(f32[16,512,128]{2,0,1:T(8,128)} %get-tuple-element.317, f32[1,512,128]{2,0,1:T(1,128)S(1)} %bitcast.89, s32[]{:T(128)S(6)} %copy.52, s32[]{:T(128)} %constant.87.clone.1..sunk, s32[]{:T(128)} %constant.87.clone.1..sunk) | dynamic-update-slice | bytes 524292 | tf_op jit(solution)/shard_map/while/body/jit(dynamic_update_index_in_dim)/dynamic_update_slice | solution.py:95
  468.3 6.5 %bitcast_reduce_fusion = f32[8,1536,128]{2,1,0:T(8,128)S(1)} fusion(f32[16,1536,128]{2,1,0:T(8,128)} %get-tuple-element.135), kind=kLoop, calls=%fused_computation.45 | loop fusion | flops 1572864 | bytes 18874368 | tf_op jit(solution)/shard_map/reduce_sum | solution.py:103
  478.1 6.5 %bitcast_reduce_fusion.1 = f32[8,1536,128]{2,1,0:T(8,128)S(1)} fusion(f32[16,1536,128]{2,1,0:T(8,128)} %get-tuple-element.134), kind=kLoop, calls=%fused_computation.46 | loop fusion | flops 1572864 | bytes 18874368 | tf_op jit(solution)/shard_map/reduce_sum | solution.py:100
  486.1 16.3 %collective-permute-done.6 = f32[512,8,128]{2,0,1:T(8,128)} collective-permute-done((f32[512,8,128]{2,0,1:T(8,128)}, f32[512,8,128]{2,0,1:T(8,128)}, u32[]{:S(2)}, u32[]{:S(2)}) %collective-permute-start.6) | collective-permute-done | bytes 2097184 | tf_op jit(solution)/shard_map/ppermute | solution.py:16
  512.4 13.2 %fusion.47 = (f32[128]{0:T(128)S(1)}, f32[512,16]{1,0:T(8,128)S(1)}) fusion(bf16[512,16,128]{2,1,0:T(8,128)(2,1)S(1)} %copy-done.1, f32[16,512,128]{2,0,1:T(8,128)S(1)} %copy-done.3, f32[512,16]{1,0:T(8,128)S(1)} %add_rsqrt_fusion, f32[128]{0:T(128)S(1)} %copy-done.7), kind=kLoop, calls=%fused_computation.58 | loop fusion | flops 7331712 | bytes 6358016 | tf_op jit(solution)/shard_map/reduce_sum | solution.py:31
  536.1 16.2 %collective-permute-done.5 = f32[512,8,128]{2,0,1:T(8,128)S(1)} collective-permute-done((f32[512,8,128]{2,0,1:T(8,128)S(1)}, f32[512,8,128]{2,0,1:T(8,128)S(1)}, u32[]{:S(2)}, u32[]{:S(2)}) %collective-permute-start.5) | collective-permute-done | bytes 2097184 | tf_op jit(solution)/shard_map/ppermute | solution.py:16
  556.7 79.6 %all-reduce = (f32[128]{0:T(128)}, f32[128]{0:T(128)}) all-reduce(f32[128]{0:T(128)S(1)} %get-tuple-element.202, f32[128]{0:T(128)S(1)} %get-tuple-element.200), channel_id=1, replica_groups=mesh['seq'=16,'head'=2] {'seq','head'}, use_global_device_ids=true, to_apply=%region_11.12 | all-reduce | flops 256 | bytes 2048 | tf_op jit(solution)/shard_map/psum | solution.py:114
  (204 shorter events, 306.1 us)
Async XLA Ops:
  0.6 12.3 %copy-start.4 = (bf16[512,8,128]{2,1,0:T(8,128)(2,1)S(1)}, bf16[512,8,128]{2,1,0:T(8,128)(2,1)}, u32[]{:S(2)}) copy-start(bf16[512,8,128]{2,1,0:T(8,128)(2,1)} %param.9) | copy-start | bytes 3145732
  0.6 12.3 %copy-start.8 = (f32[128]{0:T(128)S(1)}, f32[128]{0:T(128)}, u32[]{:S(2)}) copy-start(f32[128]{0:T(128)} %param.13) | copy-start | bytes 1540
  0.7 20.5 %copy-start = (bf16[512,16,128]{2,1,0:T(8,128)(2,1)S(1)}, bf16[512,16,128]{2,1,0:T(8,128)(2,1)}, u32[]{:S(2)}) copy-start(bf16[512,16,128]{2,1,0:T(8,128)(2,1)} %param.8) | copy-start | bytes 6291460
  3.1 19.2 %copy-start.7 = (f32[128]{0:T(128)S(1)}, f32[128]{0:T(128)}, u32[]{:S(2)}) copy-start(f32[128]{0:T(128)} %param.12) | copy-start | bytes 1540
  3.1 26.0 %collective-permute-start.3 = (bf16[512,8,128]{2,0,1:T(8,128)(2,1)}, bf16[512,8,128]{2,0,1:T(8,128)(2,1)}, u32[]{:S(2)}, u32[]{:S(2)}) collective-permute-start(bf16[512,8,128]{2,0,1:T(8,128)(2,1)} %copy.23), channel_id=1, source_target_pairs={{0,2},{2,4},{4,6},{6,8},{8,10},{10,12},{12,14},{14,16},{16,18},{18... | collective-permute-start | bytes 3145736 | tf_op jit(solution)/shard_map/ppermute | solution.py:16
  6.6 27.4 %collective-permute-start.2 = (bf16[512,8,128]{2,0,1:T(8,128)(2,1)}, bf16[512,8,128]{2,0,1:T(8,128)(2,1)}, u32[]{:S(2)}, u32[]{:S(2)}) collective-permute-start(bf16[512,8,128]{2,0,1:T(8,128)(2,1)} %copy.23), channel_id=1, source_target_pairs={{0,4},{2,6},{4,8},{6,10},{8,12},{10,14},{12,16},{14,18},{16,20},{1... | collective-permute-start | bytes 3145736 | tf_op jit(solution)/shard_map/ppermute | solution.py:16
  14.5 22.7 %collective-permute-start.1 = (bf16[512,8,128]{2,0,1:T(8,128)(2,1)}, bf16[512,8,128]{2,0,1:T(8,128)(2,1)}, u32[]{:S(2)}, u32[]{:S(2)}) collective-permute-start(bf16[512,8,128]{2,0,1:T(8,128)(2,1)} %fusion.53), channel_id=1, source_target_pairs={{0,2},{2,4},{4,6},{6,8},{8,10},{10,12},{12,14},{14,16},{16,18},{18... | collective-permute-start | bytes 3145736 | tf_op jit(solution)/shard_map/ppermute | solution.py:16
  18.7 37.8 %collective-permute-start = (bf16[512,8,128]{2,0,1:T(8,128)(2,1)}, bf16[512,8,128]{2,0,1:T(8,128)(2,1)}, u32[]{:S(2)}, u32[]{:S(2)}) collective-permute-start(bf16[512,8,128]{2,0,1:T(8,128)(2,1)} %fusion.53), channel_id=1, source_target_pairs={{0,4},{2,6},{4,8},{6,10},{8,12},{10,14},{12,16},{14,18},{16,20},{1... | collective-permute-start | bytes 3145736 | tf_op jit(solution)/shard_map/ppermute | solution.py:16
  91.0 2.2 copy-start.9
  116.5 2.2 copy-start.9
  142.0 2.2 copy-start.9
  193.1 2.2 copy-start.9
  218.6 2.2 copy-start.9
  244.2 2.2 copy-start.9
  269.8 2.2 copy-start.9
  423.1 2.2 copy-start.9
  474.8 3.3 copy-start.2
  476.5 25.9 %collective-permute-start.6 = (f32[512,8,128]{2,0,1:T(8,128)}, f32[512,8,128]{2,0,1:T(8,128)}, u32[]{:S(2)}, u32[]{:S(2)}) collective-permute-start(f32[512,8,128]{2,0,1:T(8,128)} %slice.27), channel_id=1, source_target_pairs={{2,0},{4,2},{6,4},{8,6},{10,8},{12,10},{14,12},{16,14},{18,16},{20... | collective-permute-start | bytes 6291464 | tf_op jit(solution)/shard_map/ppermute | solution.py:16
  484.8 26.0 %collective-permute-start.4 = (f32[512,8,128]{2,0,1:T(8,128)S(1)}, f32[512,8,128]{2,0,1:T(8,128)S(1)}, u32[]{:S(2)}, u32[]{:S(2)}) collective-permute-start(f32[512,8,128]{2,0,1:T(8,128)S(1)} %slice.24), channel_id=1, source_target_pairs={{2,0},{4,2},{6,4},{8,6},{10,8},{12,10},{14,12},{16,14},{18,16},{20... | collective-permute-start | bytes 6291464 | tf_op jit(solution)/shard_map/ppermute | solution.py:16
  504.8 7.6 %copy-start.1 = (bf16[512,16,128]{2,1,0:T(8,128)(2,1)S(1)}, bf16[512,16,128]{2,1,0:T(8,128)(2,1)}, u32[]{:S(2)}) copy-start(bf16[512,16,128]{2,1,0:T(8,128)(2,1)} %param.8) | copy-start | bytes 6291460
  504.8 7.6 %copy-start.3 = (f32[16,512,128]{2,0,1:T(8,128)S(1)}, f32[16,512,128]{2,0,1:T(8,128)}, u32[]{:S(2)}) copy-start(f32[16,512,128]{2,0,1:T(8,128)} %get-tuple-element.133) | copy-start | bytes 12582916
  504.8 27.7 %collective-permute-start.7 = (f32[512,8,128]{2,0,1:T(8,128)S(1)}, f32[512,8,128]{2,0,1:T(8,128)S(1)}, u32[]{:S(2)}, u32[]{:S(2)}) collective-permute-start(f32[512,8,128]{2,0,1:T(8,128)S(1)} %slice_add_fusion.1), channel_id=1, source_target_pairs={{2,0},{4,2},{6,4},{8,6},{10,8},{12,10},{14,12},{16,14},{18,16},{20... | collective-permute-start | bytes 6291464 | tf_op jit(solution)/shard_map/ppermute | solution.py:16
  511.1 41.3 %collective-permute-start.5 = (f32[512,8,128]{2,0,1:T(8,128)S(1)}, f32[512,8,128]{2,0,1:T(8,128)S(1)}, u32[]{:S(2)}, u32[]{:S(2)}) collective-permute-start(f32[512,8,128]{2,0,1:T(8,128)S(1)} %slice_add_fusion.3), channel_id=1, source_target_pairs={{2,0},{4,2},{6,4},{8,6},{10,8},{12,10},{14,12},{16,14},{18,16},{20... | collective-permute-start | bytes 6291464 | tf_op jit(solution)/shard_map/ppermute | solution.py:16
  530.4 22.0 %copy-start.5 = (bf16[512,8,128]{2,1,0:T(8,128)(2,1)S(1)}, bf16[512,8,128]{2,1,0:T(8,128)(2,1)}, u32[]{:S(2)}) copy-start(bf16[512,8,128]{2,1,0:T(8,128)(2,1)} %param.9) | copy-start | bytes 3145732
  (9 other events, 19.8 us)
where the time goes:
time: 642 us; the launch traced here: 636 us
  matrix products  228 us (36%)
  local copies, waits for them, and re-layouts  151 us (24%)
  blocking collectives  79.6 us (12%)
  waiting for transfers between devices  63.4 us (10%)
  other arithmetic  51 us (8%)
  loops' own time  42.3 us (7%)
  starting transfers between devices  20.2 us (3%)
    dynamic_update_slice x16, local copies, waits for them, and re-layouts, per_device(): lax.scan(per_head, 0, (head_ids, query_heads, upstream_heads))  129 us
    psum x1, blocking collectives, per_device(): lax.psum((q_gain_part, k_gain_part), ('seq', 'head'))  79.6 us
    ppermute x8, waiting for transfers between devices, passed_along(): lax.ppermute(value, axis, [(source, source + steps) for source in range(i...  63.4 us
    dot_general x16, matrix products, head_grads(): lax.dot_general(probs_low, incoming_gradient, first_first, preferred_elem...  56.1 us
    another operation x1, loops' own time, per_device(): lax.scan(per_head, 0, (head_ids, query_heads, upstream_heads))  42.3 us
    dot_general x16, matrix products, head_grads(): lax.dot_general(query_head, key_head, last_last, preferred_element_type=j...  42.1 us
    dot_general x16, matrix products, head_grads(): lax.dot_general(d_scores, query_head, first_first, preferred_element_type...  38.6 us
    dot_general x16, matrix products, head_grads(): jnp.dot(probs_low, value_head, preferred_element_type=jnp.float32)  35.7 us
  transfers between devices with their start and end apart: 8, of which 6 were waited for; matrix products, arithmetic and copies ran while one was open for 7% of the time, Pallas kernels for 0%

commit v1 on v0

v1 whole, which is shorter than its diff:
```python
import functools

import jax
import jax.numpy as jnp
from jax import lax
from jax.experimental import pallas as pl
from jax.experimental.pallas import tpu as pltpu
from jax.sharding import PartitionSpec as P

WINDOW = 1024
TILE = 128

score_scale = 168.0 ** (-0.5)
norm_eps = 1e-06
exp2_scale = score_scale * 1.4426950408889634

NT = (((1,), (1,)), ((), ()))


def inverse_rms_of(as_float):
    return lax.rsqrt(jnp.mean(as_float * as_float, axis=-1, keepdims=True) + norm_eps)


def norm_back(d_normed, raw, inverse_rms, gain_vec):
    unit_rows = raw * inverse_rms
    d_unit = d_normed * gain_vec
    return inverse_rms * (
        d_unit - unit_rows * jnp.mean(d_unit * unit_rows, axis=-1, keepdims=True)
    )


def heads_kernel(
    shard_ref, q_ref, g_ref, own_ref, near_ref, far_ref, q_gain_ref, k_gain_ref,
    dq_ref, d_own_ref, d_near_ref, d_far_ref, gains_ref,
    k_low, k_low_t, values, q_low, probs_all, d_scores_all,
):
    rows = own_ref.shape[2]
    group = q_ref.shape[1] // rows
    lanes = TILE * group
    blocks = rows // TILE
    tiles = WINDOW // TILE
    q_gain, k_gain = q_gain_ref[...], k_gain_ref[...]
    far_ok = jnp.where(shard_ref[0] >= 2, 1.0, 0.0)
    near_ok = jnp.where(shard_ref[0] >= 1, 1.0, 0.0)
    key_refs = (far_ref, near_ref, own_ref)

    @pl.when(pl.program_id(0) == 0)
    def _():
        gains_ref[...] = jnp.zeros_like(gains_ref)

    for place, ref in enumerate(key_refs):
        raw = ref[0, 0].astype(jnp.float32)
        here = slice(place * rows, (place + 1) * rows)
        k_low[here, :] = (raw * inverse_rms_of(raw) * k_gain).astype(jnp.bfloat16)
        values[here, :] = ref[0, 1]
    k_low_t[...] = k_low[...].T
    raw_q = q_ref[0].astype(jnp.float32)
    q_low[...] = (raw_q * inverse_rms_of(raw_q) * q_gain).astype(jnp.bfloat16)

    key_ids = lax.broadcasted_iota(jnp.int32, (TILE, lanes), 0)
    token_ids = lax.broadcasted_iota(jnp.int32, (TILE, lanes), 1) // group
    late = key_ids <= token_ids
    edge_ok = jnp.where(late, 1.0, far_ok)
    q_gain_sum = jnp.zeros_like(q_gain)

    for block in range(blocks):
        span = slice(block * TILE, block * TILE + WINDOW + TILE)
        mine = slice(block * lanes, (block + 1) * lanes)
        scores = lax.dot_general(
            k_low[span, :], q_low[mine, :], NT, preferred_element_type=jnp.float32
        )
        scores = jnp.concatenate(
            [jnp.where(late, scores[WINDOW:], scores[:TILE]), scores[TILE:WINDOW]], axis=0
        )
        exp_scores = jnp.exp2(scores * exp2_scale)
        edge = exp_scores[:TILE] * edge_ok
        first_near = (blocks - block) * TILE
        first_own = first_near + rows
        total = jnp.sum(edge, axis=0, keepdims=True)
        for low, high, ok in (
            (TILE, first_near, far_ok),
            (first_near, min(first_own, WINDOW), near_ok),
            (first_own, WINDOW, None),
        ):
            if low < high:
                part = jnp.sum(exp_scores[low:high], axis=0, keepdims=True)
                total = total + (part if ok is None else part * ok)
        inverse = 1.0 / total
        probs = jnp.concatenate([edge, exp_scores[TILE:]], axis=0) * inverse
        d_probs = lax.dot_general(
            values[span, :], g_ref[0, mine, :], NT, preferred_element_type=jnp.float32
        )
        d_probs = jnp.concatenate(
            [jnp.where(late, d_probs[WINDOW:], d_probs[:TILE]), d_probs[TILE:WINDOW]], axis=0
        )
        offset = jnp.sum(probs * d_probs, axis=0, keepdims=True)
        d_scores = probs * (d_probs - offset)
        for whole, held in ((probs, probs_all), (d_scores, d_scores_all)):
            start = block * TILE
            held[start : start + TILE, mine] = jnp.where(late, 0.0, whole[:TILE]).astype(
                jnp.bfloat16
            )
            held[start + TILE : start + WINDOW, mine] = whole[TILE:].astype(jnp.bfloat16)
            held[start + WINDOW : start + WINDOW + TILE, mine] = jnp.where(
                late, whole[:TILE], 0.0
            ).astype(jnp.bfloat16)
        query_grad = score_scale * jnp.dot(
            k_low_t[:, span], d_scores_all[span, mine], preferred_element_type=jnp.float32
        ).T
        raw = q_ref[0, mine, :].astype(jnp.float32)
        inverse_rms = inverse_rms_of(raw)
        q_gain_sum = q_gain_sum + jnp.sum(query_grad * (raw * inverse_rms), axis=0, keepdims=True)
        dq_ref[0, mine, :] = norm_back(query_grad, raw, inverse_rms, q_gain).astype(dq_ref.dtype)

    pieces = [(tile, tile + 1, 0, tile + 1) for tile in range(blocks - 1)]
    pieces += [(blocks - 1, tiles + 1, 0, blocks)]
    pieces += [(tiles + block, tiles + block + 1, block, blocks) for block in range(1, blocks)]
    k_gain_sum = jnp.zeros_like(k_gain)
    for first, last, low, high in pieces:
        meets = slice(low * lanes, high * lanes)
        keys = slice(first * TILE, last * TILE)
        value_grad = jnp.dot(
            probs_all[keys, meets], g_ref[0, meets, :], preferred_element_type=jnp.float32
        )
        key_grad = score_scale * jnp.dot(
            d_scores_all[keys, meets], q_low[meets, :], preferred_element_type=jnp.float32
        )
        for place, (ref, out) in enumerate(
            ((far_ref, d_far_ref), (near_ref, d_near_ref), (own_ref, d_own_ref))
        ):
            start = max(first * TILE, place * rows)
            stop = min(last * TILE, (place + 1) * rows)
            if start >= stop:
                continue
            inside = slice(start - place * rows, stop - place * rows)
            here = slice(start - first * TILE, stop - first * TILE)
            raw = ref[0, 0, inside, :].astype(jnp.float32)
            k_gain_sum = k_gain_sum + jnp.sum(
                key_grad[here] * (raw * inverse_rms_of(raw)), axis=0, keepdims=True
            )
            out[0, 0, inside, :] = key_grad[here].astype(out.dtype)
            out[0, 1, inside, :] = value_grad[here].astype(out.dtype)
    gains_ref[0:1, :] += q_gain_sum
    gains_ref[1:2, :] += k_gain_sum


def group_grads(shard, first, queries, grads, own, near, far, q_gain, k_gain):
    count, _, rows, width = near.shape
    query_rows = queries.shape[1]
    span = WINDOW + rows
    whole_q = pl.BlockSpec((1, query_rows, width), lambda head: (first + head, 0, 0))
    part = pl.BlockSpec((1, 2, rows, width), lambda head: (head, 0, 0, 0))
    gain = pl.BlockSpec((1, width), lambda head: (0, 0))
    flops = 2 * 5 * count * query_rows * (WINDOW + TILE) * width
    return pl.pallas_call(
        heads_kernel,
        grid=(count,),
        in_specs=[
            pl.BlockSpec(memory_space=pltpu.SMEM),
            whole_q,
            whole_q,
            pl.BlockSpec((1, 2, rows, width), lambda head: (first + head, 0, 0, 0)),
            part,
            part,
            gain,
            gain,
        ],
        out_specs=[
            pl.BlockSpec((1, query_rows, width), lambda head: (head, 0, 0)),
            part,
            part,
            part,
            pl.BlockSpec((2, width), lambda head: (0, 0)),
        ],
        out_shape=[
            jax.ShapeDtypeStruct((count, query_rows, width), jnp.bfloat16),
            jax.ShapeDtypeStruct(near.shape, jnp.float32),
            jax.ShapeDtypeStruct(near.shape, jnp.bfloat16),
            jax.ShapeDtypeStruct(near.shape, jnp.bfloat16),
            jax.ShapeDtypeStruct((2, width), jnp.float32),
        ],
        scratch_shapes=[
            pltpu.VMEM((span, width), jnp.bfloat16),
            pltpu.VMEM((width, span), jnp.bfloat16),
            pltpu.VMEM((span, width), jnp.bfloat16),
            pltpu.VMEM((query_rows, width), jnp.bfloat16),
            pltpu.VMEM((span, query_rows), jnp.bfloat16),
            pltpu.VMEM((span, query_rows), jnp.bfloat16),
        ],
        compiler_params=pltpu.CompilerParams(vmem_limit_bytes=40 * 1024 * 1024),
        cost_estimate=pl.CostEstimate(
            flops=2 * flops,
            bytes_accessed=count * (6 * query_rows + 20 * rows) * width,
            transcendentals=count * query_rows * WINDOW,
        ),
    )(shard, queries, grads, own, near, far, q_gain, k_gain)


def group_sizes(kv_dev):
    half = (kv_dev + 1) // 2
    return [size for size in (half, kv_dev - half) if size]


def per_device(query, key, value, grad_out, q_gain, k_gain):
    rows, heads, width = query.shape
    kv_dev = key.shape[1]
    group = heads // kv_dev
    count = lax.axis_size("seq")
    assert 2 * rows == WINDOW and rows % TILE == 0 and count % 2 == 0
    shard = lax.axis_index("seq")
    odd = shard % 2 == 1
    ahead = [(source, source + 2) for source in range(count - 2)]
    back = [(source + 2, source) for source in range(count - 2)]
    swap = [(source, source ^ 1) for source in range(count)]

    def by_head(array):
        split = array.reshape(rows, kv_dev, group, width)
        return jnp.transpose(split, (1, 0, 2, 3)).reshape(kv_dev, rows * group, width)

    own = jnp.transpose(jnp.stack([key, value]), (2, 0, 1, 3))
    sizes = group_sizes(kv_dev)
    starts = [sum(sizes[:place]) for place in range(len(sizes))]
    fars = [
        lax.ppermute(own[first : first + size], "seq", ahead)
        for first, size in zip(starts, sizes, strict=True)
    ]
    queries, grads = by_head(query), by_head(grad_out)
    scalar = shard.astype(jnp.int32).reshape(1)
    gains_2d = (q_gain.reshape(1, width), k_gain.reshape(1, width))
    dq_parts, key_parts, value_parts, gain_sum = [], [], [], 0.0
    for first, size, far in zip(starts, sizes, fars, strict=True):
        mine = own[first : first + size]
        near = lax.ppermute(jnp.where(odd, far, mine), "seq", swap)
        dq, d_own, d_near, d_far, gains = group_grads(
            scalar, first, queries, grads, own, near, far, *gains_2d
        )
        swapped = lax.ppermute(d_near, "seq", swap).astype(jnp.float32)
        relayed = (d_far.astype(jnp.float32) + jnp.where(odd, swapped, 0.0)).astype(jnp.bfloat16)
        returned = lax.ppermute(relayed, "seq", back).astype(jnp.float32)
        total = d_own + returned + jnp.where(odd, 0.0, swapped)
        raw = mine[:, 0].astype(jnp.float32)
        key_grad = norm_back(total[:, 0], raw, inverse_rms_of(raw), k_gain)
        dq_parts.append(dq)
        key_parts.append(key_grad.astype(jnp.bfloat16))
        value_parts.append(total[:, 1].astype(jnp.bfloat16))
        gain_sum = gain_sum + gains
    gain_sum = jnp.sum(lax.all_gather(gain_sum, ("seq", "head")), axis=0)
    grad_query = jnp.concatenate(dq_parts).reshape(kv_dev, rows, group, width)
    grad_query = jnp.transpose(grad_query, (1, 0, 2, 3)).reshape(rows, heads, width)
    grad_key = jnp.transpose(jnp.concatenate(key_parts), (1, 0, 2))
    grad_value = jnp.transpose(jnp.concatenate(value_parts), (1, 0, 2))
    return (grad_query, grad_key, grad_value, gain_sum[0], gain_sum[1])


def solution(mesh):
    split, whole = P("seq", "head", None), P()
    return jax.shard_map(
        per_device,
        mesh=mesh,
        in_specs=(split, split, split, split, whole, whole),
        out_specs=(split, split, split, whole, whole),
        check_vma=False,
    )
```

time: 642 us -> 216 us (0.34)
  matrix products: 228 us -> 0 us
  local copies, waits for them, and re-layouts: 151 us -> 14 us
  Pallas kernels: 0 us -> 42.6 us
  loops' own time: 42.3 us -> 0 us
  other arithmetic: 51 us -> 10.9 us
  waiting for transfers between devices: 63.4 us -> 41 us
  blocking collectives: 79.6 us -> 92.5 us
  starting transfers between devices: 20.2 us -> 13.4 us
    dot_general x96 -> x0, matrix products: 228 us -> none  [the longest x16 56.1 us: head_grads(): lax.dot_general(probs_low, incoming_gradient, first_first, preferred_elem...]
    dynamic_update_slice x16 -> x0, local copies, waits for them, and re-layouts: 129 us -> none  [per_device(): lax.scan(per_head, 0, (head_ids, query_heads, upstream_heads))]
    all_gather x0 -> x1, blocking collectives: none -> 92.5 us  [per_device(): gain_sum = jnp.sum(lax.all_gather(gain_sum, ('seq', 'head')), axis=0)]
    psum x1 -> x0, blocking collectives: 79.6 us -> none  [per_device(): lax.psum((q_gain_part, k_gain_part), ('seq', 'head'))]
    pallas_call x0 -> x2, Pallas kernels: none -> 42.6 us  [group_grads(): pl.pallas_call(heads_kernel, grid=(count,), in_specs=[pl.BlockSpec(memory...]
    another operation x1 -> x0, loops' own time: 42.3 us -> none  [per_device(): lax.scan(per_head, 0, (head_ids, query_heads, upstream_heads))]
    reduce_sum x6 -> x3, other arithmetic: 30.5 us -> 1.98 us  [the longest x1 1.32 us: norm_back(): jnp.mean(d_unit * unit_rows, axis=-1, keepdims=True)]
    ppermute x8, waiting for transfers between devices: 63.4 us -> 41 us  [the longest x2 40.9 us: per_device(): lax.ppermute(own[first:first + size], 'seq', ahead)]
  transfers between devices with their start and end apart: 8 -> 8, of which waited for: 6 -> 2; matrix products, arithmetic and copies ran while one was open for 7% -> 6% of each run, Pallas kernels for 0% -> 20%
where the time goes in v1:
time: 216 us; the launch traced here: 215 us
  blocking collectives  92.5 us (43%)
  Pallas kernels  42.6 us (20%)
  waiting for transfers between devices  41 us (19%)
  local copies, waits for them, and re-layouts  14 us (6%)
  starting transfers between devices  13.4 us (6%)
  other arithmetic  10.9 us (5%)
    all_gather x1, blocking collectives, per_device(): gain_sum = jnp.sum(lax.all_gather(gain_sum, ('seq', 'head')), axis=0)  92.5 us
    pallas_call x2, Pallas kernels, group_grads(): pl.pallas_call(heads_kernel, grid=(count,), in_specs=[pl.BlockSpec(memory...  42.6 us
    ppermute x2, waiting for transfers between devices, per_device(): lax.ppermute(own[first:first + size], 'seq', ahead)  40.9 us
    ppermute x2, starting transfers between devices, per_device(): lax.ppermute(own[first:first + size], 'seq', ahead)  9.4 us
    unnamed x21, local copies, waits for them, and re-layouts  4.51 us
  transfers between devices with their start and end apart: 8, of which 2 were waited for; matrix products, arithmetic and copies ran while one was open for 6% of the time, Pallas kernels for 20%

profile of v1, /device:TPU:0, one launch (start us, length us, event | category | flops | bytes accessed | tf_op | source)
XLA Modules:
  0.0 215.4 jit_solution(17124012146407656526)
XLA Ops:
  0.6 1.9 copy_bitcast_fusion
  2.8 1.0 slice.47
  3.8 4.9 %collective-permute-start.2 = (bf16[4,2,512,128]{3,2,1,0:T(8,128)(2,1)}, bf16[4,2,512,128]{3,2,1,0:T(8,128)(2,1)S(1)}, u32[]{:S(2)}, u32[]{:S(2)}) collective-permute-start(bf16[4,2,512,128]{3,2,1,0:T(8,128)(2,1)} %slice.47), channel_id=1, source_target_pairs={{0,4},{2,6},{4,8},{6,10},{8,12},{10,14},{12,16},{14,18},{16,20},{1... | collective-permute-start | bytes 3145736 | tf_op jit(solution)/shard_map/ppermute | solution.py:224
  8.8 22.6 %collective-permute-done.2.far_ref = bf16[4,2,512,128]{3,2,1,0:T(8,128)(2,1)S(1)} collective-permute-done((bf16[4,2,512,128]{3,2,1,0:T(8,128)(2,1)}, bf16[4,2,512,128]{3,2,1,0:T(8,128)(2,1)S(1)}, u32[]{:S(2)}, u32[]{:S(2)}) %collective-permute-start.2) | collective-permute-done | bytes 1048608 | tf_op jit(solution)/shard_map/ppermute | solution.py:224
  31.7 4.5 %collective-permute-start = (bf16[4,2,512,128]{3,2,0,1:T(8,128)(2,1)S(1)}, bf16[4,2,512,128]{3,2,0,1:T(8,128)(2,1)S(1)}, u32[]{:S(2)}, u32[]{:S(2)}) collective-permute-start(bf16[4,2,512,128]{3,2,0,1:T(8,128)(2,1)S(1)} %copy.47), channel_id=1, source_target_pairs={{0,4},{2,6},{4,8},{6,10},{8,12},{10,14},{12,16},{14,18},{16,20},{1... | collective-permute-start | bytes 3145736 | tf_op jit(solution)/shard_map/ppermute | solution.py:224
  36.2 1.4 copy.29
  37.8 1.4 copy.30
  39.3 18.3 %collective-permute-done = bf16[4,2,512,128]{3,2,0,1:T(8,128)(2,1)S(1)} collective-permute-done((bf16[4,2,512,128]{3,2,0,1:T(8,128)(2,1)S(1)}, bf16[4,2,512,128]{3,2,0,1:T(8,128)(2,1)S(1)}, u32[]{:S(2)}, u32[]{:S(2)}) %collective-permute-start) | collective-permute-done | bytes 1048608 | tf_op jit(solution)/shard_map/ppermute | solution.py:224
  57.8 21.4 %shard_map.102 = (bf16[4,1024,128]{2,1,0:T(8,128)(2,1)S(1)}, f32[4,2,512,128]{3,2,1,0:T(8,128)S(1)}, bf16[4,2,512,128]{3,2,1,0:T(8,128)(2,1)S(1)}, bf16[4,2,512,128]{3,2,1,0:T(8,128)(2,1)S(1)}, f32[2,128]{1,0:T(2,128)S(1)}) custom-call(s32[1]{0:T(128)} %bitcast.shard_ref, bf16[8,1024,128]{2,1,0:T(8,128)(2,1)S(1)} %bitcast.71, ...), custom_call_target="tpu_custom_call" | custom-call | flops 12079595520 | bytes 8388608 | tf_op jit(solution)/shard_map/pallas_call | solution.py:155
  79.9 0.6 copy-done
  80.6 21.2 %shard_map.101 = (bf16[4,1024,128]{2,1,0:T(8,128)(2,1)S(1)}, f32[4,2,512,128]{3,2,1,0:T(8,128)S(1)}, bf16[4,2,512,128]{3,2,1,0:T(8,128)(2,1)S(1)}, bf16[4,2,512,128]{3,2,1,0:T(8,128)(2,1)S(1)}, f32[2,128]{1,0:T(2,128)S(1)}) custom-call(s32[1]{0:T(128)} %bitcast.shard_ref, bf16[8,1024,128]{2,1,0:T(8,128)(2,1)S(1)} %bitcast.72, ...), custom_call_target="tpu_custom_call" | custom-call | flops 12079595520 | bytes 8388608 | tf_op jit(solution)/shard_map/pallas_call | solution.py:155
  102.4 0.6 fusion.18
  103.1 1.3 fusion.4
  104.4 1.5 collective-permute-start.7
  106.2 2.8 %copy.37 = bf16[512,8,2,128]{3,2,1,0:T(2,128)(2,1)} copy(bf16[512,8,2,128]{3,2,0,1:T(2,128)(2,1)S(1)} %bitcast.79) | data formatting | bytes 4194304 | tf_op jit(solution)/shard_map/transpose | solution.py:249
  108.9 1.3 fusion.1
  110.2 1.3 collective-permute-start.5
  111.5 92.5 %all-gather.1 = f32[32,2,128]{2,1,0:T(2,128)S(1)} all-gather(f32[1,2,128]{2,1,0:T(2,128)S(1)} %add_bitcast_fusion), channel_id=2, replica_groups=mesh['seq'=16,'head'=2] {'seq','head'}, dimensions={0}, use_global_device_ids=true | all-gather | bytes 33792 | tf_op jit(solution)/shard_map/all_gather | solution.py:247
  204.7 2.4 %fusion.5 = f32[4,2,512,128]{3,2,0,1:T(8,128)S(1)} fusion(bf16[4,2,512,128]{3,2,0,1:T(8,128)(2,1)S(1)} %collective-permute-done.6, f32[4,2,512,128]{3,2,1,0:T(8,128)} %copy-done, bf16[4,2,512,128]{3,2,0,1:T(8,128)(2,1)} %collective-permute-done.7, pred[]{:T(512)S(6)} %eq.5), kind=kLoop, calls=%fused_computation.9 | loop fusion | flops 2621440 | bytes 6291457 | tf_op jit(solution)/shard_map/add | solution.py:240
  207.5 1.6 fusion.2
  209.2 1.6 copy.46
  210.9 1.3 fusion.14
  212.2 1.4 fusion.17
  213.8 1.6 copy.45
  (47 shorter events, 3.7 us)
Async XLA Ops:
  3.8 27.6 %collective-permute-start.2 = (bf16[4,2,512,128]{3,2,1,0:T(8,128)(2,1)}, bf16[4,2,512,128]{3,2,1,0:T(8,128)(2,1)S(1)}, u32[]{:S(2)}, u32[]{:S(2)}) collective-permute-start(bf16[4,2,512,128]{3,2,1,0:T(8,128)(2,1)} %slice.47), channel_id=1, source_target_pairs={{0,4},{2,6},{4,8},{6,10},{8,12},{10,14},{12,16},{14,18},{16,20},{1... | collective-permute-start | bytes 3145736 | tf_op jit(solution)/shard_map/ppermute | solution.py:224
  31.6 4.7 %copy-start.7 = (bf16[512,16,128]{2,1,0:T(8,128)(2,1)S(1)}, bf16[512,16,128]{2,1,0:T(8,128)(2,1)}, u32[]{:S(2)}) copy-start(bf16[512,16,128]{2,1,0:T(8,128)(2,1)} %param.6) | copy-start | bytes 6291460
  31.7 25.9 %collective-permute-start = (bf16[4,2,512,128]{3,2,0,1:T(8,128)(2,1)S(1)}, bf16[4,2,512,128]{3,2,0,1:T(8,128)(2,1)S(1)}, u32[]{:S(2)}, u32[]{:S(2)}) collective-permute-start(bf16[4,2,512,128]{3,2,0,1:T(8,128)(2,1)S(1)} %copy.47), channel_id=1, source_target_pairs={{0,4},{2,6},{4,8},{6,10},{8,12},{10,14},{12,16},{14,18},{16,20},{1... | collective-permute-start | bytes 3145736 | tf_op jit(solution)/shard_map/ppermute | solution.py:224
  36.1 21.7 %collective-permute-start.3 = (bf16[4,2,512,128]{3,2,1,0:T(8,128)(2,1)S(1)}, bf16[4,2,512,128]{3,2,1,0:T(8,128)(2,1)S(1)}, u32[]{:S(2)}, u32[]{:S(2)}) collective-permute-start(bf16[4,2,512,128]{3,2,1,0:T(8,128)(2,1)S(1)} %get-tuple-element.42), channel_id=1, source_target_pairs={{0,2},{2,0},{4,6},{6,4},{8,10},{10,8},{12,14},{14,12},{16,18},{18,... | collective-permute-start | bytes 3145736 | tf_op jit(solution)/shard_map/ppermute | solution.py:233
  36.2 1.6 copy-start.8
  39.3 18.5 %copy-start.3 = (f32[128]{0:T(128)S(1)}, f32[128]{0:T(128)}, u32[]{:S(2)}) copy-start(f32[128]{0:T(128)} %param.11) | copy-start | bytes 1540
  39.3 18.5 %copy-start.4 = (f32[128]{0:T(128)S(1)}, f32[128]{0:T(128)}, u32[]{:S(2)}) copy-start(f32[128]{0:T(128)} %param.10) | copy-start | bytes 1540
  57.7 22.8 %collective-permute-start.1 = (bf16[4,2,512,128]{3,2,0,1:T(8,128)(2,1)S(1)}, bf16[4,2,512,128]{3,2,0,1:T(8,128)(2,1)S(1)}, u32[]{:S(2)}, u32[]{:S(2)}) collective-permute-start(bf16[4,2,512,128]{3,2,0,1:T(8,128)(2,1)S(1)} %broadcast_select_fusion.1), channel_id=1, source_target_pairs={{0,2},{2,0},{4,6},{6,4},{8,10},{10,8},{12,14},{14,12},{16,18},{18,... | collective-permute-start | bytes 3145736 | tf_op jit(solution)/shard_map/ppermute | solution.py:233
  79.2 1.3 copy-start
  79.3 23.8 %collective-permute-start.6 = (bf16[4,2,512,128]{3,2,0,1:T(8,128)(2,1)S(1)}, bf16[4,2,512,128]{3,2,0,1:T(8,128)(2,1)S(1)}, u32[]{:S(2)}, u32[]{:S(2)}) collective-permute-start(bf16[4,2,512,128]{3,2,0,1:T(8,128)(2,1)S(1)} %copy.43), channel_id=1, source_target_pairs={{0,2},{2,0},{4,6},{6,4},{8,10},{10,8},{12,14},{14,12},{16,18},{18,... | collective-permute-start | bytes 3145736 | tf_op jit(solution)/shard_map/ppermute | solution.py:237
  101.8 2.6 %copy-start.1 = (f32[4,2,512,128]{3,2,1,0:T(8,128)}, f32[4,2,512,128]{3,2,1,0:T(8,128)S(1)}, u32[]{:S(2)}) copy-start(f32[4,2,512,128]{3,2,1,0:T(8,128)S(1)} %get-tuple-element.17) | copy-start | bytes 6291460
  101.9 7.0 %collective-permute-start.4 = (bf16[4,2,512,128]{3,2,0,1:T(8,128)(2,1)S(1)}, bf16[4,2,512,128]{3,2,0,1:T(8,128)(2,1)S(1)}, u32[]{:S(2)}, u32[]{:S(2)}) collective-permute-start(bf16[4,2,512,128]{3,2,0,1:T(8,128)(2,1)S(1)} %copy.40), channel_id=1, source_target_pairs={{0,2},{2,0},{4,6},{6,4},{8,10},{10,8},{12,14},{14,12},{16,18},{18,... | collective-permute-start | bytes 3145736 | tf_op jit(solution)/shard_map/ppermute | solution.py:237
  104.4 100.2 %collective-permute-start.7 = (bf16[4,2,512,128]{3,2,0,1:T(8,128)(2,1)}, bf16[4,2,512,128]{3,2,0,1:T(8,128)(2,1)}, u32[]{:S(2)}, u32[]{:S(2)}) collective-permute-start(bf16[4,2,512,128]{3,2,0,1:T(8,128)(2,1)} %fusion.4), channel_id=1, source_target_pairs={{4,0},{6,2},{8,4},{10,6},{12,8},{14,10},{16,12},{18,14},{20,16},{2... | collective-permute-start | bytes 3145736 | tf_op jit(solution)/shard_map/ppermute | solution.py:239
  108.9 2.6 %copy-start.5 = (bf16[4,2,512,128]{3,2,0,1:T(8,128)(2,1)}, bf16[4,2,512,128]{3,2,0,1:T(8,128)(2,1)S(1)}, u32[]{:S(2)}) copy-start(bf16[4,2,512,128]{3,2,0,1:T(8,128)(2,1)S(1)} %collective-permute-done.4) | copy-start | bytes 3145732
  110.2 96.9 %collective-permute-start.5 = (bf16[4,2,512,128]{3,2,0,1:T(8,128)(2,1)}, bf16[4,2,512,128]{3,2,0,1:T(8,128)(2,1)}, u32[]{:S(2)}, u32[]{:S(2)}) collective-permute-start(bf16[4,2,512,128]{3,2,0,1:T(8,128)(2,1)} %fusion.1), channel_id=1, source_target_pairs={{4,0},{6,2},{8,4},{10,6},{12,8},{14,10},{16,12},{18,14},{20,16},{2... | collective-permute-start | bytes 3145736 | tf_op jit(solution)/shard_map/ppermute | solution.py:239
  204.7 2.5 %copy-start.2 = (f32[4,2,512,128]{3,2,1,0:T(8,128)S(1)}, f32[4,2,512,128]{3,2,1,0:T(8,128)}, u32[]{:S(2)}) copy-start(f32[4,2,512,128]{3,2,1,0:T(8,128)} %copy-done.1) | copy-start | bytes 6291460
  204.7 2.8 %copy-start.6 = (bf16[4,2,512,128]{3,2,0,1:T(8,128)(2,1)S(1)}, bf16[4,2,512,128]{3,2,0,1:T(8,128)(2,1)}, u32[]{:S(2)}) copy-start(bf16[4,2,512,128]{3,2,0,1:T(8,128)(2,1)} %copy-done.5) | copy-start | bytes 3145732
